TPU v7x, 32 devices: a whole 2x2x4 slice. The times are simulated.
32 devices in a mesh: ctx: 16 (over z, y, x), head: 2 (over core).
Axes of the slice: x: 2, y: 2, z: 4, core: 2. Of those that a mesh axis runs over, the one named last changes fastest.
Arguments:
- queries: bfloat16 [4096, 4096], P('ctx', 'head'), may hold values from -12 to 12
- keys: bfloat16 [4096, 4096], P('ctx', 'head'), may hold values from -4 to 4
- values: bfloat16 [4096, 4096], P('ctx', 'head'), may hold values from -6 to 6
- pool_weight: bfloat16 [128, 256], P('ctx'), may hold values from -0.375 to 0.375
- out_weight: bfloat16 [4096, 4096], P('head', 'ctx'), may hold values from -0.09375 to 0.09375
- pattern: int32 [32, 5], replicated, may hold values from 0 to 31, as said below
Outputs:
- mixed: bfloat16 [4096, 4096], P('ctx', 'head')
Inputs may be any that keep to these rules, and one draw needn't show every extreme that they name: `pattern`: the flat butterfly with the blocks of each shard relabelled: entry (i, b) names a key block that agrees with block i in all bits above b and differs from it in bit b. For b < 1 the lower bits are arbitrary. For b >= 1 the bits from 1 to b - 1 equal those of i, and over the 2 query blocks of one aligned group of 2 blocks the lowest 1 bits take each of their 2 values once.
All inputs are finite; a program needn't handle non-finite values.
Results may differ from a plain program's by a relative error of at most 0.019.
Values may be sent and summed in bfloat16 or wider, within the bound.
A program may use at most 128 MiB of HBM per device.

v0:
```python
import jax
import jax.numpy as jnp
from jax import lax
from jax.sharding import PartitionSpec as P

HEAD_DIMENSION = 128
BLK = 128


def partner_2(x, axis, stride):
    return lax.ppermute(x, axis, [(i, i ^ 1 << stride) for i in range(lax.axis_size(axis))])


def merge_scores(running, scores, value_set, einsum_form):
    old_max, row_sum, weighted = running
    row_max = jnp.maximum(old_max, jnp.max(scores, axis=-1))
    weights = jnp.exp(scores - row_max[..., None])
    rescale = jnp.exp(old_max - row_max)
    row_sum = row_sum * rescale + jnp.sum(weights, axis=-1)
    weighted = weighted * rescale[..., None] + jnp.einsum(
        einsum_form, weights.astype(jnp.bfloat16), value_set, preferred_element_type=jnp.float32
    )
    return (row_max, row_sum, weighted)


def on_device(queries, keys, values, pool_weight, out_weight, pattern):
    tok_rows, col_width = queries.shape
    local_heads = col_width // HEAD_DIMENSION
    block_count = tok_rows // BLK
    local_bits = block_count.bit_length() - 1
    remote_bits = lax.axis_size("ctx").bit_length() - 1
    score_scale = HEAD_DIMENSION ** (-0.5)
    own_index = lax.axis_index("ctx")
    own_rows = lax.dynamic_slice_in_dim(pattern, own_index * block_count, block_count, 0)
    query_blk = queries.reshape(block_count, BLK, local_heads, HEAD_DIMENSION)
    key_rows = keys.reshape(block_count, BLK, col_width)
    value_rows = values.reshape(block_count, BLK, col_width)
    running = (
        jnp.full((block_count, local_heads, BLK), -jnp.inf, jnp.float32),
        jnp.zeros((block_count, local_heads, BLK), jnp.float32),
        jnp.zeros((block_count, local_heads, BLK, HEAD_DIMENSION), jnp.float32),
    )
    near_index = jnp.concatenate(
        [
            jnp.arange(block_count, dtype=jnp.int32)[:, None],
            own_rows[:, :local_bits] - own_index * block_count,
        ],
        axis=1,
    )
    near_keys = jnp.take(key_rows, near_index, axis=0).reshape(
        block_count, -1, local_heads, HEAD_DIMENSION
    )
    near_values = jnp.take(value_rows, near_index, axis=0).reshape(
        block_count, -1, local_heads, HEAD_DIMENSION
    )
    scores = (
        jnp.einsum("bqhd,bkhd->bhqk", query_blk, near_keys, preferred_element_type=jnp.float32)
        * score_scale
    )
    running = merge_scores(running, scores, near_values, "bhqk,bkhd->bhqd")
    pooled_landmark_keys = jnp.dot(pool_weight, keys, preferred_element_type=jnp.float32).astype(
        jnp.bfloat16
    )
    pooled_landmark_values = jnp.dot(
        pool_weight, values, preferred_element_type=jnp.float32
    ).astype(jnp.bfloat16)
    piece_keys = lax.all_gather(pooled_landmark_keys, "ctx", axis=0, tiled=True).reshape(
        -1, local_heads, HEAD_DIMENSION
    )
    piece_values = lax.all_gather(pooled_landmark_values, "ctx", axis=0, tiled=True).reshape(
        -1, local_heads, HEAD_DIMENSION
    )
    mark_scores = (
        jnp.einsum("bqhd,khd->bhqk", query_blk, piece_keys, preferred_element_type=jnp.float32)
        * score_scale
    )
    running = merge_scores(running, mark_scores, piece_values, "bhqk,khd->bhqd")
    for level in range(remote_bits):
        partner = jnp.bitwise_xor(own_index, 1 << level)
        wanted = own_rows[:, local_bits + level] - partner * block_count
        recv_keys, recv_values = partner_2((key_rows, value_rows), "ctx", level)
        far_keys = jnp.take(recv_keys, wanted, axis=0)
        far_values = jnp.take(recv_values, wanted, axis=0)
        far_scores = (
            jnp.einsum(
                "bqhd,bkhd->bhqk",
                query_blk,
                far_keys.reshape(block_count, BLK, local_heads, HEAD_DIMENSION),
                preferred_element_type=jnp.float32,
            )
            * score_scale
        )
        running = merge_scores(
            running,
            far_scores,
            far_values.reshape(block_count, BLK, local_heads, HEAD_DIMENSION),
            "bhqk,bkhd->bhqd",
        )
    row_max, row_sum, weighted = running
    attended = (
        (weighted / row_sum[..., None])
        .transpose(0, 2, 1, 3)
        .reshape(tok_rows, col_width)
        .astype(jnp.bfloat16)
    )
    partial_value = jnp.dot(
        attended,
        lax.all_gather(out_weight, "ctx", axis=1, tiled=True),
        preferred_element_type=jnp.float32,
    )
    return lax.psum_scatter(
        partial_value.astype(jnp.bfloat16), "head", scatter_dimension=1, tiled=True
    )


def solution(mesh):
    in_specs = (
        P("ctx", "head"),
        P("ctx", "head"),
        P("ctx", "head"),
        P("ctx", None),
        P("head", "ctx"),
        P(),
    )
    out_specs = P("ctx", "head")
    return jax.shard_map(
        on_device, mesh=mesh, in_specs=in_specs, out_specs=out_specs, check_vma=False
    )
```

profile of v0, /device:TPU:11, one launch (start us, length us, event | category | flops | bytes accessed | tf_op | source)
XLA Modules:
  0.0 424.6 jit_solution(1723453091043764816)
XLA Ops:
  7.6 1.2 collective-permute-start.2
  8.9 1.2 collective-permute-start.1
  11.5 2.0 gather_fusion
  13.5 2.0 gather_fusion.1
  15.5 1.4 copy.210
  17.0 4.0 broadcast_select_fusion
  21.0 1.9 copy.209
  23.2 76.0 %all_gather.9 = bf16[128,2048]{1,0:T(8,128)(2,1)S(1)} all-gather(bf16[8,2048]{1,0:T(8,128)(2,1)S(1)} %convolution_convert_fusion.2), channel_id=1, replica_groups=mesh['ctx'=16,'head'=2] {'ctx'}, dimensions={0}, use_global_device_ids=true | all-gather | bytes 557056 | tf_op jit(solution)/shard_map/all_gather | solution.py:67
  99.2 0.9 copy.212
  100.3 40.3 %all_gather.10 = bf16[128,2048]{1,0:T(8,128)(2,1)} all-gather(bf16[8,2048]{1,0:T(8,128)(2,1)S(1)} %convolution_convert_fusion.1), channel_id=1, replica_groups=mesh['ctx'=16,'head'=2] {'ctx'}, dimensions={0}, use_global_device_ids=true | all-gather | bytes 557056 | tf_op jit(solution)/shard_map/all_gather | solution.py:70
  140.7 2.0 copy.207
  142.7 2.3 copy.211
  145.1 1.9 bitcast_reduce_fusion.5
  146.9 0.9 bitcast_reduce_fusion
  148.8 20.0 %collective-permute-start.6 = (bf16[2,128,2048]{2,1,0:T(8,128)(2,1)S(1)}, bf16[2,128,2048]{2,1,0:T(8,128)(2,1)}, u32[]{:S(2)}, u32[]{:S(2)}) collective-permute-start(bf16[2,128,2048]{2,1,0:T(8,128)(2,1)S(1)} %bitcast.255), channel_id=1, source_target_pairs={{0,16},{2,18},{4,20},{6,22},{8,24},{10,26},{12,28},{14,30},{16,0},... | collective-permute-start | bytes 3145736 | tf_op jit(solution)/shard_map/ppermute | solution.py:11
  168.9 2.6 fusion.3
  171.5 2.9 gather_fusion.2
  174.4 2.8 gather_fusion.3
  177.2 2.8 gather_fusion.4
  180.1 2.8 gather_fusion.5
  182.9 4.4 %broadcast_select_fusion.6 = (bf16[2,128,2048]{2,1,0:T(8,128)(2,1)}, bf16[2,128,2048]{2,1,0:T(8,128)(2,1)}, bf16[2,128,2048]{2,1,0:T(8,128)(2,1)}, bf16[2,128,2048]{2,1,0:T(8,128)(2,1)}) fusion(bf16[2,128,2048]{2,1,0:T(8,128)(2,1)} %gather_fusion.5, pred[2]{0:T(512)(128)(4,1)S(1)} %get-tuple-element.36, bf16[2,128,2048]{2,1,0:T(8,128)(2,1)} %gather_fusion.4, ...), kind=kLoop, calls=%fused_computation.85 | loop fusion | flops 2097152 | bytes 8388612 | tf_op jit(solution)/shard_map/jit(_take)/select_n | solution.py:83
  187.3 2.3 copy.169
  189.6 2.3 copy.163
  191.9 2.8 gather_fusion.6
  194.8 56.7 %collective-permute-done.5 = bf16[2,128,2048]{2,1,0:T(8,128)(2,1)} collective-permute-done((bf16[2,128,2048]{2,1,0:T(8,128)(2,1)S(1)}, bf16[2,128,2048]{2,1,0:T(8,128)(2,1)}, u32[]{:S(2)}, u32[]{:S(2)}) %collective-permute-start.5) | collective-permute-done | bytes 1048608 | tf_op jit(solution)/shard_map/ppermute | solution.py:11
  251.4 2.8 gather_fusion.7
  254.3 3.5 collective-permute-done.6
  257.7 2.9 gather_fusion.8
  260.6 65.5 %collective-permute-done.7 = bf16[2,128,2048]{2,1,0:T(8,128)(2,1)} collective-permute-done((bf16[2,128,2048]{2,1,0:T(8,128)(2,1)S(1)}, bf16[2,128,2048]{2,1,0:T(8,128)(2,1)}, u32[]{:S(2)}, u32[]{:S(2)}) %collective-permute-start.7) | collective-permute-done | bytes 1048608 | tf_op jit(solution)/shard_map/ppermute | solution.py:11
  326.2 2.9 gather_fusion.9
  329.1 3.7 broadcast_select_fusion.2
  332.8 2.3 copy.181
  335.1 1.3 copy.175
  336.5 2.2 bitcast_reduce_fusion.3
  338.7 2.2 bitcast_reduce_fusion.4
  340.9 2.2 bitcast_reduce_fusion.1
  343.1 2.3 bitcast_reduce_fusion.2
  345.4 2.4 copy.166
  347.7 1.4 copy.172
  349.1 1.6 copy.178
  350.7 2.3 copy.184
  353.0 2.1 fusion.24
  359.9 0.9 fusion.37
  361.1 0.9 fusion.35
  362.0 0.9 fusion.33
  363.9 5.0 %fusion.6 = bf16[2,128,16,128]{3,1,2,0:T(8,128)(2,1)S(1)} fusion(f32[2,16,128,128]{3,2,1,0:T(8,128)S(1)} %fusion.33, f32[2,16,128,128]{3,2,1,0:T(8,128)S(1)} %fusion.35, f32[2,16,128,128]{3,2,1,0:T(8,128)S(1)} %fusion.37, f32[16,128,2,128]{1,3,0,2:T(8,128)S(1)} %fusion.41, f32[2,16,128,128]{3,2,1,0:T(8,128)S(1)} %copy-done.20, ...), kind=kOutput, calls=%fused_computation.21 | convolution fusion | flops 142606336 | bytes 14811136 | tf_op jit(solution)/shard_map/bhqk,bkhd->bhqd/dot_general | solution.py:20
  369.6 11.7 %convolution_convert_fusion = bf16[256,4096]{1,0:T(8,128)(2,1)} fusion(bf16[2048,4096]{1,0:T(8,128)(2,1)} %all-gather.2.cloned.1.call-done, bf16[32,8,16,128]{3,2,1,0:T(8,128)(2,1)S(1)} %bitcast.279), kind=kOutput, calls=%fused_computation.10 | convolution fusion | flops 4296015872 | bytes 19922944 | tf_op jit(solution)/shard_map/dot_general | solution.py:106
  381.4 36.3 %reduce-scatter.2.cloned.1.call-done = bf16[256,2048]{1,0:T(8,128)(2,1)} async-done(((bf16[256,4096]{1,0:T(8,128)(2,1)}), bf16[256,2048]{1,0:T(8,128)(2,1)}) %reduce-scatter.2.cloned.1.call-update) | async-done | bytes 1048592 | tf_op jit(solution)/shard_map/reduce_scatter | solution.py:111
  (85 shorter events, 10.8 us)
Async XLA Ops:
  6.5 16.4 %copy-start = (bf16[8,256]{1,0:T(8,128)(2,1)S(1)}, bf16[8,256]{1,0:T(8,128)(2,1)}, u32[]{:S(2)}) copy-start(bf16[8,256]{1,0:T(8,128)(2,1)} %param.13) | copy-start | bytes 12292
  6.5 4.9 %copy-start.4 = (bf16[256,2048]{1,0:T(8,128)(2,1)S(1)}, bf16[256,2048]{1,0:T(8,128)(2,1)}, u32[]{:S(2)}) copy-start(bf16[256,2048]{1,0:T(8,128)(2,1)} %param.11) | copy-start | bytes 3145732
  6.5 363.1 %all-gather.2.cloned.1.call-start = ((), (), s32[]{:S(2)}) async-start(), calls=%async_computation.1 | async-start | bytes 17825792 | tf_op jit(solution)/shard_map/all_gather | solution.py:108
  7.3 410.5 %reduce-scatter.2.cloned.1.call-start = ((), (), s32[]{:S(2)}) async-start(), calls=%async_computation.2 | async-start | bytes 3145728 | tf_op jit(solution)/shard_map/reduce_scatter | solution.py:111
  7.3 141.4 %collective-permute-start = (bf16[2,128,2048]{2,1,0:T(8,128)(2,1)}, bf16[2,128,2048]{2,1,0:T(8,128)(2,1)}, u32[]{:S(2)}, u32[]{:S(2)}) collective-permute-start(bf16[2,128,2048]{2,1,0:T(8,128)(2,1)} %bitcast.251), channel_id=1, source_target_pairs={{0,2},{2,0},{4,6},{6,4},{8,10},{10,8},{12,14},{14,12},{16,18},{18,... | collective-permute-start | bytes 3145736 | tf_op jit(solution)/shard_map/ppermute | solution.py:11
  7.6 161.2 %collective-permute-start.2 = (bf16[2,128,2048]{2,1,0:T(8,128)(2,1)}, bf16[2,128,2048]{2,1,0:T(8,128)(2,1)}, u32[]{:S(2)}, u32[]{:S(2)}) collective-permute-start(bf16[2,128,2048]{2,1,0:T(8,128)(2,1)} %bitcast.252), channel_id=1, source_target_pairs={{0,4},{2,6},{4,0},{6,2},{8,12},{10,14},{12,8},{14,10},{16,20},{18,... | collective-permute-start | bytes 3145736 | tf_op jit(solution)/shard_map/ppermute | solution.py:11
  8.9 139.9 %collective-permute-start.1 = (bf16[2,128,2048]{2,1,0:T(8,128)(2,1)}, bf16[2,128,2048]{2,1,0:T(8,128)(2,1)}, u32[]{:S(2)}, u32[]{:S(2)}) collective-permute-start(bf16[2,128,2048]{2,1,0:T(8,128)(2,1)} %bitcast.256), channel_id=1, source_target_pairs={{0,2},{2,0},{4,6},{6,4},{8,10},{10,8},{12,14},{14,12},{16,18},{18,... | collective-permute-start | bytes 3145736 | tf_op jit(solution)/shard_map/ppermute | solution.py:11
  10.1 170.0 %collective-permute-start.3 = (bf16[2,128,2048]{2,1,0:T(8,128)(2,1)}, bf16[2,128,2048]{2,1,0:T(8,128)(2,1)}, u32[]{:S(2)}, u32[]{:S(2)}) collective-permute-start(bf16[2,128,2048]{2,1,0:T(8,128)(2,1)} %bitcast.257), channel_id=1, source_target_pairs={{0,4},{2,6},{4,0},{6,2},{8,12},{10,14},{12,8},{14,10},{16,20},{18,... | collective-permute-start | bytes 3145736 | tf_op jit(solution)/shard_map/ppermute | solution.py:11
  10.3 181.6 %collective-permute-start.4 = (bf16[2,128,2048]{2,1,0:T(8,128)(2,1)}, bf16[2,128,2048]{2,1,0:T(8,128)(2,1)}, u32[]{:S(2)}, u32[]{:S(2)}) collective-permute-start(bf16[2,128,2048]{2,1,0:T(8,128)(2,1)} %bitcast.253), channel_id=1, source_target_pairs={{0,8},{2,10},{4,12},{6,14},{8,0},{10,2},{12,4},{14,6},{16,24},{18,... | collective-permute-start | bytes 3145736 | tf_op jit(solution)/shard_map/ppermute | solution.py:11
  11.4 2.0 copy-start.5
  142.7 2.4 copy-start.19
  145.0 2.0 copy-start.7
  148.7 102.7 %collective-permute-start.5 = (bf16[2,128,2048]{2,1,0:T(8,128)(2,1)S(1)}, bf16[2,128,2048]{2,1,0:T(8,128)(2,1)}, u32[]{:S(2)}, u32[]{:S(2)}) collective-permute-start(bf16[2,128,2048]{2,1,0:T(8,128)(2,1)S(1)} %bitcast.259), channel_id=1, source_target_pairs={{0,8},{2,10},{4,12},{6,14},{8,0},{10,2},{12,4},{14,6},{16,24},{18,... | collective-permute-start | bytes 3145736 | tf_op jit(solution)/shard_map/ppermute | solution.py:11
  148.8 109.0 %collective-permute-start.6 = (bf16[2,128,2048]{2,1,0:T(8,128)(2,1)S(1)}, bf16[2,128,2048]{2,1,0:T(8,128)(2,1)}, u32[]{:S(2)}, u32[]{:S(2)}) collective-permute-start(bf16[2,128,2048]{2,1,0:T(8,128)(2,1)S(1)} %bitcast.255), channel_id=1, source_target_pairs={{0,16},{2,18},{4,20},{6,22},{8,24},{10,26},{12,28},{14,30},{16,0},... | collective-permute-start | bytes 3145736 | tf_op jit(solution)/shard_map/ppermute | solution.py:11
  168.8 157.3 %collective-permute-start.7 = (bf16[2,128,2048]{2,1,0:T(8,128)(2,1)S(1)}, bf16[2,128,2048]{2,1,0:T(8,128)(2,1)}, u32[]{:S(2)}, u32[]{:S(2)}) collective-permute-start(bf16[2,128,2048]{2,1,0:T(8,128)(2,1)S(1)} %bitcast.260), channel_id=1, source_target_pairs={{0,16},{2,18},{4,20},{6,22},{8,24},{10,26},{12,28},{14,30},{16,0},... | collective-permute-start | bytes 3145736 | tf_op jit(solution)/shard_map/ppermute | solution.py:11
  257.7 71.3 %copy-start.9 = (bf16[2,128,2048]{2,1,0:T(8,128)(2,1)S(1)}, bf16[2,128,2048]{2,1,0:T(8,128)(2,1)}, u32[]{:S(2)}) copy-start(bf16[2,128,2048]{2,1,0:T(8,128)(2,1)} %gather_fusion.6) | copy-start | bytes 3145732
  326.2 2.9 copy-start.10
  332.8 2.3 copy-start.14
  336.5 2.2 copy-start.15
  338.7 2.2 copy-start.17
  340.9 2.2 copy-start.16
  345.4 2.4 copy-start.11
  353.0 2.6 copy-start.3
  355.1 1.6 copy-start.8
  355.6 1.9 copy-start.6
  357.2 1.1 copy-start.18
  358.0 1.6 copy-start.2
  358.0 1.9 copy-start.13
  359.9 1.2 copy-start.12
  362.0 1.6 copy-start.20
  362.0 1.9 copy-start.21
  369.6 48.1 %copy-start.1 = (bf16[8,256]{1,0:T(8,128)(2,1)S(1)}, bf16[8,256]{1,0:T(8,128)(2,1)}, u32[]{:S(2)}) copy-start(bf16[8,256]{1,0:T(8,128)(2,1)} %param.13) | copy-start | bytes 12292
Sparse Core Ops, SparseCore 0:
  10.1 341.5 all-gather.1
  381.5 36.1 reduce-scatter.1
where the time goes:
time: 426 us; the launch traced here: 425 us
  waiting for transfers between devices  163 us (38%)
  blocking collectives  116 us (27%)
  local copies, waits for them, and re-layouts  56.7 us (13%)
  matrix products  34.7 us (8%)
  starting transfers between devices  23.4 us (5%)
  other arithmetic  17 us (4%)
  between operations  13.7 us (3%)
    ppermute x8, waiting for transfers between devices, partner_2(): lax.ppermute(x, axis, [(i, i ^ 1 << stride) for i in range(lax.axis_size(...  126 us
    all_gather x1, blocking collectives, on_device(): lax.all_gather(pooled_landmark_keys, 'ctx', axis=0, tiled=True)  76 us
    all_gather x1, blocking collectives, on_device(): lax.all_gather(pooled_landmark_values, 'ctx', axis=0, tiled=True)  40.3 us
    reduce_scatter x1, waiting for transfers between devices, on_device(): lax.psum_scatter(partial_value.astype(jnp.bfloat16), 'head', scatter_dime...  36.3 us
    ppermute x8, starting transfers between devices, partner_2(): lax.ppermute(x, axis, [(i, i ^ 1 << stride) for i in range(lax.axis_size(...  23.3 us
    dot_general x1, matrix products, on_device(): jnp.dot(attended, lax.all_gather(out_weight, 'ctx', axis=1, tiled=True),...  11.7 us
    gather x4, local copies, waits for them, and re-layouts, on_device(): far_keys = jnp.take(recv_keys, wanted, axis=0)  11.5 us
    gather x4, local copies, waits for them, and re-layouts, on_device(): far_values = jnp.take(recv_values, wanted, axis=0)  11.3 us
  transfers between devices with their start and end apart: 10, of which 4 were waited for; matrix products, arithmetic and copies ran while one was open for 22% of the time, Pallas kernels for 0%

commit v1 on v0

v1 whole, which is shorter than its diff:
```python
import functools

import jax
import jax.numpy as jnp
from jax import lax
from jax.experimental import pallas as pl
from jax.experimental.pallas import tpu as pltpu
from jax.sharding import PartitionSpec as P

HEAD_DIMENSION = 128
BLK = 128
NEAR_LEVELS = 1
MESH = pl.DeviceIdType.MESH
PIECES = 2


def flip_bit(index, step):
    return index + step - 2 * step * lax.rem(lax.div(index, step), 2)


def differing_bits(first, second, steps):
    total = 0
    for step in steps:
        a = lax.rem(lax.div(first, step), 2)
        b = lax.rem(lax.div(second, step), 2)
        total = total + step * (a + b - 2 * a * b)
    return total


def scores_of(queries, keys):
    return lax.dot_general(
        queries, keys, (((1,), (1,)), ((), ())), preferred_element_type=jnp.float32
    )


def layer_kernel(n_ctx, n_head, *refs):
    steps = [1 << bit for bit in range(n_ctx.bit_length() - 1)]
    levels = len(steps)
    q_ref, k_ref, v_ref, pool_ref, w_ref, pattern_ref, out_ref = refs[:7]
    refs = refs[7:]
    far_k, refs = refs[:levels], refs[levels:]
    far_v, refs = refs[:levels], refs[levels:]
    (w_buf, marks, acc, top, total, attended, partial, arrived) = refs[:8]
    (kv_send, kv_recv, w_send, w_recv, mark_send, mark_recv, head_send, head_recv, own_sem) = refs[8:]

    tok_rows, col_width = q_ref.shape
    heads = col_width // HEAD_DIMENSION
    blocks = tok_rows // BLK
    land = pool_ref.shape[0]
    depth, w_width = w_ref.shape
    piece_rows = depth // PIECES
    scale = HEAD_DIMENSION ** (-0.5)

    me = lax.axis_index("ctx")
    my_head = lax.axis_index("head")
    partner = {step: flip_bit(me, step) for step in steps}
    head_peer = [lax.rem(my_head + j, n_head) for j in range(n_head)]

    barrier = pltpu.get_barrier_semaphore()
    for step in steps:
        pl.semaphore_signal(barrier, inc=1, device_id={"ctx": partner[step]}, device_id_type=MESH)
    for j in range(1, n_head):
        pl.semaphore_signal(barrier, inc=1, device_id={"head": head_peer[j]}, device_id_type=MESH)
    pl.semaphore_wait(barrier, levels + n_head - 1)

    descending = steps[::-1]
    orders = [descending, descending[:-2] + descending[-2:][::-1]]

    held = [[[0]] for _ in orders]
    for order, stages in zip(orders, held):
        for step in order:
            before = [r for stage in stages for r in stage]
            stages.append([r ^ step for r in before])
    open_sends = []

    def send_w(piece, r, stage):
        step = orders[piece][stage]
        rows = pl.ds(piece * piece_rows, piece_rows)
        source = w_ref.at[rows] if r == 0 else w_buf.at[r, rows]
        copy = pltpu.make_async_remote_copy(
            src_ref=source,
            dst_ref=w_buf.at[r ^ step, rows],
            send_sem=w_send.at[piece, r, stage],
            recv_sem=w_recv.at[piece, r ^ step],
            device_id={"ctx": partner[step]},
            device_id_type=MESH,
        )
        copy.start()
        open_sends.append(copy)

    def wait_w(piece, r):
        rows = pl.ds(piece * piece_rows, piece_rows)
        pltpu.make_async_remote_copy(
            src_ref=w_ref.at[rows],
            dst_ref=w_buf.at[r, rows],
            send_sem=w_send.at[piece, 0, 0],
            recv_sem=w_recv.at[piece, r],
            device_id={"ctx": partner[1]},
            device_id_type=MESH,
        ).wait_recv()

    def forward_w(stage):
        for index in range(len(held[0][stage + 1])):
            for piece in range(PIECES):
                r = held[piece][stage + 1][index]
                wait_w(piece, r)
                for later in range(stage + 1, levels):
                    send_w(piece, r, later)

    kv_copies = {}

    def send_kv(level):
        copies = []
        for which, (source, target) in enumerate(((k_ref, far_k[level]), (v_ref, far_v[level]))):
            copy = pltpu.make_async_remote_copy(
                src_ref=source,
                dst_ref=target,
                send_sem=kv_send.at[level, which],
                recv_sem=kv_recv.at[level, which],
                device_id={"ctx": partner[steps[level]]},
                device_id_type=MESH,
            )
            copy.start()
            copies.append(copy)
        kv_copies[level] = copies

    mark_copies = []

    def send_marks(stage):
        size = 1 << stage
        copy = pltpu.make_async_remote_copy(
            src_ref=marks.at[pl.ds(0, size)],
            dst_ref=marks.at[pl.ds(size, size)],
            send_sem=mark_send.at[stage],
            recv_sem=mark_recv.at[stage],
            device_id={"ctx": partner[size]},
            device_id_type=MESH,
        )
        copy.start()
        mark_copies.append(copy)

    def head_columns(head):
        return pl.ds(pl.multiple_of(head * HEAD_DIMENSION, HEAD_DIMENSION), HEAD_DIMENSION)

    def merge(head, rows, raw, value_set):
        old_top = top[head, rows]
        new_top = jnp.maximum(old_top, jnp.max(raw, axis=-1, keepdims=True))
        weights = jnp.exp((raw - new_top) * scale)
        rescale = jnp.exp((old_top - new_top) * scale)
        total[head, rows] = total[head, rows] * rescale + jnp.sum(weights, axis=-1, keepdims=True)
        acc[head, rows] = acc[head, rows] * rescale + jnp.dot(
            weights.astype(jnp.bfloat16), value_set, preferred_element_type=jnp.float32
        )
        top[head, rows] = new_top

    def near_attention():
        @pl.loop(0, heads)
        def _(head):
            columns = head_columns(head)
            raw = scores_of(q_ref[:, columns], k_ref[:, columns])
            row_top = jnp.max(raw, axis=-1, keepdims=True)
            weights = jnp.exp((raw - row_top) * scale)
            top[head] = row_top
            total[head] = jnp.sum(weights, axis=-1, keepdims=True)
            acc[head] = jnp.dot(
                weights.astype(jnp.bfloat16), v_ref[:, columns], preferred_element_type=jnp.float32
            )

    def mark_attention():
        @pl.loop(0, heads)
        def _(head):
            columns = head_columns(head)
            both = marks[:, :, columns].astype(jnp.float32)
            mark_keys = both[:, :land].reshape(n_ctx * land, HEAD_DIMENSION).astype(jnp.bfloat16)
            mark_values = both[:, land:].reshape(n_ctx * land, HEAD_DIMENSION).astype(jnp.bfloat16)
            merge(head, pl.ds(0, tok_rows), scores_of(q_ref[:, columns], mark_keys), mark_values)

    def chosen(ref, wanted, columns):
        picked = ref[pl.ds(0, BLK), columns]
        for block in range(1, blocks):
            other = ref[pl.ds(block * BLK, BLK), columns]
            picked = lax.select(wanted == block, other, picked)
        return picked

    def far_attention(level):
        first = partner[steps[level]] * blocks
        for copy in kv_copies[level]:
            copy.wait_recv()

        @pl.loop(0, heads)
        def _(head):
            columns = head_columns(head)
            for block in range(blocks):
                wanted = pattern_ref[me * blocks + block, NEAR_LEVELS + level] - first
                rows = pl.ds(block * BLK, BLK)
                far_keys = chosen(far_k[level], wanted, columns)
                far_values = chosen(far_v[level], wanted, columns)
                merge(head, rows, scores_of(q_ref[rows, columns], far_keys), far_values)

    for piece in range(PIECES):
        send_w(piece, 0, 0)
    pooled = [
        jnp.dot(pool_ref[...], ref[...], preferred_element_type=jnp.float32) for ref in (k_ref, v_ref)
    ]
    marks[0] = jnp.concatenate(pooled, axis=0).astype(jnp.bfloat16)
    send_marks(0)
    for level in range(min(2, levels)):
        send_kv(level)
    for stage in range(1, levels):
        for piece in range(PIECES):
            send_w(piece, 0, stage)
    own_copy = pltpu.make_async_copy(w_ref, w_buf.at[0], own_sem.at[0])
    own_copy.start()

    near_attention()
    forward_w(0)
    for level in range(min(2, levels), levels)[::-1]:
        send_kv(level)
    mark_copies[0].wait_recv()
    send_marks(1)
    forward_w(1)
    far_attention(0)
    mark_copies[1].wait_recv()
    for stage in range(2, levels):
        send_marks(stage)
        if stage < levels - 1:
            forward_w(stage)
        far_attention(stage - 1)
        mark_copies[stage].wait_recv()
    mark_attention()
    far_attention(levels - 1)
    forward_w(levels - 1)

    @pl.loop(0, heads)
    def _(head):
        attended[:, head_columns(head)] = (acc[head] / total[head]).astype(jnp.bfloat16)

    own_copy.wait()
    pair = max(1, 128 // w_width)
    share = n_ctx // n_head

    def project(target, row_slot):
        @pl.loop(0, share // pair)
        def _(index):
            parts = []
            for extra in range(pair):
                slot = target * share + index * pair + extra
                r = differing_bits(slot, me, steps)
                parts.append(
                    jnp.dot(attended[...], w_buf[r], preferred_element_type=jnp.float32)
                )
            width = pair * w_width
            whole = parts[0] if pair == 1 else jnp.concatenate(parts, axis=1)
            columns = pl.ds(pl.multiple_of(index * width, width), width)
            partial[row_slot, :, columns] = whole.astype(jnp.bfloat16)

    head_copies = []
    for j in range(1, n_head):
        project(head_peer[j], j)
        copy = pltpu.make_async_remote_copy(
            src_ref=partial.at[j],
            dst_ref=arrived.at[j - 1],
            send_sem=head_send.at[j - 1],
            recv_sem=head_recv.at[j - 1],
            device_id={"head": head_peer[j]},
            device_id_type=MESH,
        )
        copy.start()
        head_copies.append(copy)
    project(my_head, 0)
    for copy in head_copies:
        copy.wait_recv()

    rows_at_once = 32

    @pl.loop(0, tok_rows // rows_at_once)
    def _(index):
        rows = pl.ds(pl.multiple_of(index * rows_at_once, rows_at_once), rows_at_once)
        mixed = partial[0, rows].astype(jnp.float32)
        for j in range(1, n_head):
            mixed += arrived[j - 1, rows].astype(jnp.float32)
        out_ref[rows] = mixed.astype(jnp.bfloat16)

    for copy in open_sends + mark_copies + head_copies:
        copy.wait_send()
    for level in range(levels):
        for copy in kv_copies[level]:
            copy.wait_send()


def on_device(n_ctx, n_head, queries, keys, values, pool_weight, out_weight, pattern):
    tok_rows, col_width = queries.shape
    heads = col_width // HEAD_DIMENSION
    depth, w_width = out_weight.shape
    land = pool_weight.shape[0]
    levels = n_ctx.bit_length() - 1
    share = n_ctx * w_width // n_head
    bf16 = jnp.bfloat16
    in_vmem = pl.BlockSpec(memory_space=pltpu.VMEM)
    return pl.pallas_call(
        functools.partial(layer_kernel, n_ctx, n_head),
        out_shape=jax.ShapeDtypeStruct((tok_rows, share), bf16),
        in_specs=[in_vmem] * 5 + [pl.BlockSpec(memory_space=pltpu.SMEM)],
        out_specs=in_vmem,
        scratch_shapes=[pltpu.VMEM((tok_rows, col_width), bf16)] * (2 * levels)
        + [
            pltpu.VMEM((n_ctx, depth, w_width), bf16),
            pltpu.VMEM((n_ctx, 2 * land, col_width), bf16),
            pltpu.VMEM((heads, tok_rows, HEAD_DIMENSION), jnp.float32),
            pltpu.VMEM((heads, tok_rows, 1), jnp.float32),
            pltpu.VMEM((heads, tok_rows, 1), jnp.float32),
            pltpu.VMEM((tok_rows, col_width), bf16),
            pltpu.VMEM((n_head, tok_rows, share), bf16),
            pltpu.VMEM((n_head - 1, tok_rows, share), bf16),
            pltpu.SemaphoreType.DMA((levels, 2)),
            pltpu.SemaphoreType.DMA((levels, 2)),
            pltpu.SemaphoreType.DMA((PIECES, n_ctx, levels)),
            pltpu.SemaphoreType.DMA((PIECES, n_ctx)),
            pltpu.SemaphoreType.DMA((levels,)),
            pltpu.SemaphoreType.DMA((levels,)),
            pltpu.SemaphoreType.DMA((n_head - 1,)),
            pltpu.SemaphoreType.DMA((n_head - 1,)),
            pltpu.SemaphoreType.DMA((1,)),
        ],
        compiler_params=pltpu.CompilerParams(
            collective_id=0, has_side_effects=True, vmem_limit_bytes=56 * 1024 * 1024
        ),
    )(queries, keys, values, pool_weight, out_weight, pattern)


def solution(mesh):
    in_specs = (
        P("ctx", "head"),
        P("ctx", "head"),
        P("ctx", "head"),
        P("ctx", None),
        P("head", "ctx"),
        P(),
    )
    out_specs = P("ctx", "head")
    body = functools.partial(on_device, mesh.shape["ctx"], mesh.shape["head"])
    return jax.shard_map(
        body, mesh=mesh, in_specs=in_specs, out_specs=out_specs, check_vma=False
    )
```

time: 426 us -> 230 us (0.54)
  the two profiles are of different devices: /device:TPU:11 before, /device:TPU:0 now
where the time goes in v1:
time: 230 us
  Pallas kernels  226 us (98%)
  local copies, waits for them, and re-layouts  3.68 us (2%)
    pallas_call x1, Pallas kernels, on_device(): pl.pallas_call(functools.partial(layer_kernel, n_ctx, n_head), out_shape=...  226 us

profile of v1, /device:TPU:0, one launch (start us, length us, event | category | flops | bytes accessed | tf_op | source)
XLA Modules:
  0.0 230.2 jit_solution(11664951189975082741)
XLA Ops:
  0.0 1.4 copy.7.refs_5_
  1.4 226.5 %shard_map.64 = bf16[256,2048]{1,0:T(8,128)(2,1)} custom-call(bf16[256,2048]{1,0:T(8,128)(2,1)} %refs_0_.1, bf16[256,2048]{1,0:T(8,128)(2,1)} %refs_1_.1, bf16[256,2048]{1,0:T(8,128)(2,1)} %refs_2_.1, bf16[8,256]{1,0:T(8,128)(2,1)} %refs_3_.1, bf16[2048,256]{1,0:T(8,128)(2,1)} %refs_4_.1, s32[32,5]{1,0:T(8,128)} %copy.7.refs_5_), custom_call_target="tpu_custom_call" | custom-call | tf_op jit(solution)/shard_map/pallas_call | solution.py:300
  227.9 2.3 %copy.9 = bf16[256,2048]{1,0:T(8,128)(2,1)} copy(bf16[256,2048]{1,0:T(8,128)(2,1)} %shard_map.64) | data formatting | bytes 2097152

commit v2 on v1

v2 whole, which is shorter than its diff:
```python
import functools

import jax
import jax.numpy as jnp
from jax import lax
from jax.experimental import pallas as pl
from jax.experimental.pallas import tpu as pltpu
from jax.sharding import PartitionSpec as P

HEAD_DIMENSION = 128
BLK = 128
NEAR_LEVELS = 1
MESH = pl.DeviceIdType.MESH
PIECES = 2
GROUP = 4


def flip_bit(index, step):
    return index + step - 2 * step * lax.rem(lax.div(index, step), 2)


def differing_bits(first, second, steps):
    total = 0
    for step in steps:
        a = lax.rem(lax.div(first, step), 2)
        b = lax.rem(lax.div(second, step), 2)
        total = total + step * (a + b - 2 * a * b)
    return total


def scores_of(queries, keys):
    return lax.dot_general(
        queries, keys, (((1,), (1,)), ((), ())), preferred_element_type=jnp.float32
    )


def layer_kernel(n_ctx, n_head, *refs):
    steps = [1 << bit for bit in range(n_ctx.bit_length() - 1)]
    levels = len(steps)
    q_ref, k_ref, v_ref, pool_ref, w_ref, pattern_ref, out_ref = refs[:7]
    refs = refs[7:]
    far_k, refs = refs[:levels], refs[levels:]
    far_v, refs = refs[:levels], refs[levels:]
    (w_buf, marks, acc, top, total, attended, partial, arrived, summed, shared) = refs[:10]
    (kv_send, kv_recv, w_send, w_recv, mark_send, mark_recv) = refs[10:16]
    (att_send, att_recv, head_send, head_recv, out_send, out_recv) = refs[16:]

    tok_rows, col_width = q_ref.shape
    heads = col_width // HEAD_DIMENSION
    blocks = tok_rows // BLK
    land = pool_ref.shape[0]
    depth, w_width = w_ref.shape
    piece_rows = depth // PIECES
    scale = HEAD_DIMENSION ** (-0.5)

    me = lax.axis_index("ctx")
    my_head = lax.axis_index("head")
    partner = {step: flip_bit(me, step) for step in steps}
    head_peer = [lax.rem(my_head + j, n_head) for j in range(n_head)]

    barrier = pltpu.get_barrier_semaphore()
    for step in steps:
        pl.semaphore_signal(barrier, inc=1, device_id={"ctx": partner[step]}, device_id_type=MESH)
    across = flip_bit(partner[1], 2)
    member = [me, partner[1], partner[2], across]
    pl.semaphore_signal(barrier, inc=1, device_id={"ctx": across}, device_id_type=MESH)
    for j in range(1, n_head):
        pl.semaphore_signal(barrier, inc=1, device_id={"head": head_peer[j]}, device_id_type=MESH)
    pl.semaphore_wait(barrier, levels + n_head)

    order = steps[2:][::-1]
    held = [[0]]
    for step in order:
        before = [r for stage in held for r in stage]
        held.append([r ^ step for r in before])
    open_sends = []

    def send_w(piece, r, stage):
        step = order[stage]
        rows = pl.ds(piece * piece_rows, piece_rows)
        source = w_ref.at[rows] if r == 0 else w_buf.at[r // GROUP, rows]
        copy = pltpu.make_async_remote_copy(
            src_ref=source,
            dst_ref=w_buf.at[(r ^ step) // GROUP, rows],
            send_sem=w_send.at[piece, r // GROUP, stage],
            recv_sem=w_recv.at[piece, (r ^ step) // GROUP],
            device_id={"ctx": partner[step]},
            device_id_type=MESH,
        )
        copy.start()
        open_sends.append(copy)

    def wait_w(piece, r):
        rows = pl.ds(piece * piece_rows, piece_rows)
        pltpu.make_async_remote_copy(
            src_ref=w_ref.at[rows],
            dst_ref=w_buf.at[r // GROUP, rows],
            send_sem=w_send.at[piece, 0, 0],
            recv_sem=w_recv.at[piece, r // GROUP],
            device_id={"ctx": partner[1]},
            device_id_type=MESH,
        ).wait_recv()

    def forward_w(stage):
        for r in held[stage + 1]:
            for piece in range(PIECES):
                wait_w(piece, r)
                for later in range(stage + 1, len(order)):
                    send_w(piece, r, later)

    kv_copies = {}

    def send_kv(level, which):
        source, target = ((k_ref, far_k[level]), (v_ref, far_v[level]))[which]
        copy = pltpu.make_async_remote_copy(
            src_ref=source,
            dst_ref=target,
            send_sem=kv_send.at[level, which],
            recv_sem=kv_recv.at[level, which],
            device_id={"ctx": partner[steps[level]]},
            device_id_type=MESH,
        )
        copy.start()
        kv_copies[level, which] = copy

    mark_copies = []

    def send_marks(stage):
        size = 1 << stage
        copy = pltpu.make_async_remote_copy(
            src_ref=marks.at[pl.ds(0, size)],
            dst_ref=marks.at[pl.ds(size, size)],
            send_sem=mark_send.at[stage],
            recv_sem=mark_recv.at[stage],
            device_id={"ctx": partner[steps[levels - 1 - stage]]},
            device_id_type=MESH,
        )
        copy.start()
        mark_copies.append(copy)

    def head_columns(head):
        return pl.ds(pl.multiple_of(head * HEAD_DIMENSION, HEAD_DIMENSION), HEAD_DIMENSION)

    def merge(head, rows, raw, value_set):
        old_top = top[head, rows]
        new_top = jnp.maximum(old_top, jnp.max(raw, axis=-1, keepdims=True))
        weights = jnp.exp((raw - new_top) * scale)
        rescale = jnp.exp((old_top - new_top) * scale)
        total[head, rows] = total[head, rows] * rescale + jnp.sum(weights, axis=-1, keepdims=True)
        acc[head, rows] = acc[head, rows] * rescale + jnp.dot(
            weights.astype(jnp.bfloat16), value_set, preferred_element_type=jnp.float32
        )
        top[head, rows] = new_top

    def near_attention():
        @pl.loop(0, heads)
        def _(head):
            columns = head_columns(head)
            raw = scores_of(q_ref[:, columns], k_ref[:, columns])
            row_top = jnp.max(raw, axis=-1, keepdims=True)
            weights = jnp.exp((raw - row_top) * scale)
            top[head] = row_top
            total[head] = jnp.sum(weights, axis=-1, keepdims=True)
            acc[head] = jnp.dot(
                weights.astype(jnp.bfloat16), v_ref[:, columns], preferred_element_type=jnp.float32
            )

    def mark_attention():
        @pl.loop(0, heads)
        def _(head):
            columns = head_columns(head)
            both = marks[:, :, columns].astype(jnp.float32)
            mark_keys = both[:, :land].reshape(n_ctx * land, HEAD_DIMENSION).astype(jnp.bfloat16)
            mark_values = both[:, land:].reshape(n_ctx * land, HEAD_DIMENSION).astype(jnp.bfloat16)
            merge(head, pl.ds(0, tok_rows), scores_of(q_ref[:, columns], mark_keys), mark_values)

    def chosen(ref, wanted, columns):
        picked = ref[pl.ds(0, BLK), columns]
        for block in range(1, blocks):
            other = ref[pl.ds(block * BLK, BLK), columns]
            picked = lax.select(wanted == block, other, picked)
        return picked

    def far_attention(level):
        first = partner[steps[level]] * blocks
        for which in range(2):
            if (level, which) != (levels - 1, 0):
                kv_copies[level, which].wait_recv()

        @pl.loop(0, heads)
        def _(head):
            columns = head_columns(head)
            for block in range(blocks):
                wanted = pattern_ref[me * blocks + block, NEAR_LEVELS + level] - first
                rows = pl.ds(block * BLK, BLK)
                far_keys = chosen(far_k[level], wanted, columns)
                far_values = chosen(far_v[level], wanted, columns)
                merge(head, rows, scores_of(q_ref[rows, columns], far_keys), far_values)

    half = col_width // 2
    att_copies = {}

    def send_attended(source, piece, step):
        columns = pl.ds(piece * half, half)
        copy = pltpu.make_async_remote_copy(
            src_ref=attended.at[source, :, columns],
            dst_ref=attended.at[source ^ step, :, columns],
            send_sem=att_send.at[source ^ step, piece],
            recv_sem=att_recv.at[source ^ step, piece],
            device_id={"ctx": partner[step]},
            device_id_type=MESH,
        )
        copy.start()
        att_copies[source ^ step, piece] = copy

    pooled = [
        jnp.dot(pool_ref[...], ref[...], preferred_element_type=jnp.float32) for ref in (k_ref, v_ref)
    ]
    marks[0] = jnp.concatenate(pooled, axis=0).astype(jnp.bfloat16)
    send_marks(0)
    for which in range(2):
        for level in range(levels)[::-1]:
            send_kv(level, which)

    near_attention()
    mark_copies[0].wait_recv()
    send_marks(1)
    far_attention(0)
    far_attention(1)
    kv_copies[levels - 1, 0].wait_recv()
    for stage in range(len(order)):
        for piece in range(PIECES):
            send_w(piece, 0, stage)
    for stage in range(2, levels):
        mark_copies[stage - 1].wait_recv()
        send_marks(stage)
        far_attention(levels + 1 - stage)
    mark_copies[levels - 1].wait_recv()
    mark_attention()

    @pl.loop(0, heads)
    def _(head):
        attended[0, :, head_columns(head)] = (acc[head] / total[head]).astype(jnp.bfloat16)

    for piece in range(2):
        for step in (1 << piece, 2 >> piece):
            send_attended(0, piece, step)
    for piece in range(2):
        att_copies[1 << piece, piece].wait_recv()
        send_attended(1 << piece, piece, 2 >> piece)
    for stage in range(len(order) - 1):
        forward_w(stage)
    for piece in range(2):
        att_copies[2 >> piece, piece].wait_recv()
        att_copies[3, piece].wait_recv()

    turns = n_ctx // GROUP
    share = turns // n_head

    def project(r):
        turn = lax.div(differing_bits(me, r, steps), GROUP)

        @pl.loop(0, GROUP)
        def _(index):
            columns = w_ref[...] if r == 0 else w_buf[r // GROUP]
            rows = jnp.dot(attended[index], columns, preferred_element_type=jnp.float32)
            partial[index, turn] = rows.astype(jnp.bfloat16)

    for stage in range(len(order)):
        for r in held[stage]:
            project(r)
    for r in held[len(order)]:
        for piece in range(PIECES):
            wait_w(piece, r)
        project(r)

    head_copies = {}
    for index in range(GROUP)[::-1]:
        for j in range(1, n_head):
            copy = pltpu.make_async_remote_copy(
                src_ref=partial.at[index, pl.ds(head_peer[j] * share, share)],
                dst_ref=arrived.at[j - 1, index],
                send_sem=head_send.at[j - 1, index],
                recv_sem=head_recv.at[j - 1, index],
                device_id={"head": head_peer[j]},
                device_id_type=MESH,
            )
            copy.start()
            head_copies[index, j] = copy
    out_copies = []
    for index in range(GROUP)[::-1]:
        for j in range(1, n_head):
            head_copies[index, j].wait_recv()
        target = summed if index else shared
        for turn in range(share):
            mixed = partial[index, my_head * share + turn].astype(jnp.float32)
            for j in range(1, n_head):
                mixed += arrived[j - 1, index, turn].astype(jnp.float32)
            target[index, turn] = mixed.astype(jnp.bfloat16)
        if index:
            copy = pltpu.make_async_remote_copy(
                src_ref=summed.at[index],
                dst_ref=shared.at[index],
                send_sem=out_send.at[index],
                recv_sem=out_recv.at[index],
                device_id={"ctx": member[index]},
                device_id_type=MESH,
            )
            copy.start()
            out_copies.append(copy)
    for copy in out_copies:
        copy.wait_recv()

    pair = max(1, 128 // w_width)
    for first in range(0, share * GROUP, pair):
        parts = []
        for slot in range(first, first + pair):
            index = differing_bits(lax.rem(me, GROUP), slot % GROUP, (1, 2))
            parts.append(shared[index, slot // GROUP])
        whole = parts[0] if pair == 1 else jnp.concatenate(parts, axis=1)
        out_ref[:, pl.ds(first * w_width, pair * w_width)] = whole

    sent = open_sends + mark_copies + out_copies
    for copies in (kv_copies, att_copies, head_copies):
        sent.extend(copies.values())
    for copy in sent:
        copy.wait_send()


def on_device(n_ctx, n_head, queries, keys, values, pool_weight, out_weight, pattern):
    tok_rows, col_width = queries.shape
    heads = col_width // HEAD_DIMENSION
    depth, w_width = out_weight.shape
    land = pool_weight.shape[0]
    levels = n_ctx.bit_length() - 1
    turns = n_ctx // GROUP
    share = turns // n_head
    bf16 = jnp.bfloat16
    in_vmem = pl.BlockSpec(memory_space=pltpu.VMEM)
    return pl.pallas_call(
        functools.partial(layer_kernel, n_ctx, n_head),
        out_shape=jax.ShapeDtypeStruct((tok_rows, share * GROUP * w_width), bf16),
        in_specs=[in_vmem] * 5 + [pl.BlockSpec(memory_space=pltpu.SMEM)],
        out_specs=in_vmem,
        scratch_shapes=[pltpu.VMEM((tok_rows, col_width), bf16)] * (2 * levels)
        + [
            pltpu.VMEM((turns, depth, w_width), bf16),
            pltpu.VMEM((n_ctx, 2 * land, col_width), bf16),
            pltpu.VMEM((heads, tok_rows, HEAD_DIMENSION), jnp.float32),
            pltpu.VMEM((heads, tok_rows, 1), jnp.float32),
            pltpu.VMEM((heads, tok_rows, 1), jnp.float32),
            pltpu.VMEM((GROUP, tok_rows, col_width), bf16),
            pltpu.VMEM((GROUP, turns, tok_rows, w_width), bf16),
            pltpu.VMEM((n_head - 1, GROUP, share, tok_rows, w_width), bf16),
            pltpu.VMEM((GROUP, share, tok_rows, w_width), bf16),
            pltpu.VMEM((GROUP, share, tok_rows, w_width), bf16),
            pltpu.SemaphoreType.DMA((levels, 2)),
            pltpu.SemaphoreType.DMA((levels, 2)),
            pltpu.SemaphoreType.DMA((PIECES, turns, levels)),
            pltpu.SemaphoreType.DMA((PIECES, turns)),
            pltpu.SemaphoreType.DMA((levels,)),
            pltpu.SemaphoreType.DMA((levels,)),
            pltpu.SemaphoreType.DMA((GROUP, 2)),
            pltpu.SemaphoreType.DMA((GROUP, 2)),
            pltpu.SemaphoreType.DMA((n_head - 1, GROUP)),
            pltpu.SemaphoreType.DMA((n_head - 1, GROUP)),
            pltpu.SemaphoreType.DMA((GROUP,)),
            pltpu.SemaphoreType.DMA((GROUP,)),
        ],
        compiler_params=pltpu.CompilerParams(
            collective_id=0, has_side_effects=True, vmem_limit_bytes=56 * 1024 * 1024
        ),
    )(queries, keys, values, pool_weight, out_weight, pattern)


def solution(mesh):
    in_specs = (
        P("ctx", "head"),
        P("ctx", "head"),
        P("ctx", "head"),
        P("ctx", None),
        P("head", "ctx"),
        P(),
    )
    out_specs = P("ctx", "head")
    body = functools.partial(on_device, mesh.shape["ctx"], mesh.shape["head"])
    return jax.shard_map(
        body, mesh=mesh, in_specs=in_specs, out_specs=out_specs, check_vma=False
    )
```

time: 230 us -> 206 us (0.90)
  the two profiles are of different devices: /device:TPU:0 before, /device:TPU:11 now
where the time goes in v2:
time: 206 us
  Pallas kernels  202 us (98%)
  local copies, waits for them, and re-layouts  3.68 us (2%)
    pallas_call x1, Pallas kernels, on_device(): pl.pallas_call(functools.partial(layer_kernel, n_ctx, n_head), out_shape=...  202 us

profile of v2, /device:TPU:11, one launch (start us, length us, event | category | flops | bytes accessed | tf_op | source)
XLA Modules:
  0.0 205.6 jit_solution(230077711160073068)
XLA Ops:
  0.0 1.4 copy.7.refs_5_
  1.4 201.9 %shard_map.64 = bf16[256,2048]{1,0:T(8,128)(2,1)} custom-call(bf16[256,2048]{1,0:T(8,128)(2,1)} %refs_0_.1, bf16[256,2048]{1,0:T(8,128)(2,1)} %refs_1_.1, bf16[256,2048]{1,0:T(8,128)(2,1)} %refs_2_.1, bf16[8,256]{1,0:T(8,128)(2,1)} %refs_3_.1, bf16[2048,256]{1,0:T(8,128)(2,1)} %refs_4_.1, s32[32,5]{1,0:T(8,128)} %copy.7.refs_5_), custom_call_target="tpu_custom_call" | custom-call | tf_op jit(solution)/shard_map/pallas_call | solution.py:340
  203.3 2.3 %copy.9 = bf16[256,2048]{1,0:T(8,128)(2,1)} copy(bf16[256,2048]{1,0:T(8,128)(2,1)} %shard_map.64) | data formatting | bytes 2097152

commit v3 on v2

--- a/solution.py
+++ b/solution.py
@@ -11,7 +11,7 @@
 BLK = 128
 NEAR_LEVELS = 1
 MESH = pl.DeviceIdType.MESH
-PIECES = 2
+PIECES = 4
 GROUP = 4
 
 
@@ -141,38 +141,57 @@
     def head_columns(head):
         return pl.ds(pl.multiple_of(head * HEAD_DIMENSION, HEAD_DIMENSION), HEAD_DIMENSION)
 
-    def merge(head, rows, raw, value_set):
-        old_top = top[head, rows]
-        new_top = jnp.maximum(old_top, jnp.max(raw, axis=-1, keepdims=True))
-        weights = jnp.exp((raw - new_top) * scale)
-        rescale = jnp.exp((old_top - new_top) * scale)
-        total[head, rows] = total[head, rows] * rescale + jnp.sum(weights, axis=-1, keepdims=True)
-        acc[head, rows] = acc[head, rows] * rescale + jnp.dot(
-            weights.astype(jnp.bfloat16), value_set, preferred_element_type=jnp.float32
-        )
-        top[head, rows] = new_top
+    def merge(entries):
+        merged = []
+        for head, rows, raw, value_set in entries:
+            old_top = top[head, rows]
+            new_top = jnp.maximum(old_top, jnp.max(raw, axis=-1, keepdims=True))
+            weights = jnp.exp((raw - new_top) * scale)
+            rescale = jnp.exp((old_top - new_top) * scale)
+            new_total = total[head, rows] * rescale + jnp.sum(weights, axis=-1, keepdims=True)
+            new_acc = acc[head, rows] * rescale + jnp.dot(
+                weights.astype(jnp.bfloat16), value_set, preferred_element_type=jnp.float32
+            )
+            merged.append((new_top, new_total, new_acc))
+        for (head, rows, _, _), (new_top, new_total, new_acc) in zip(entries, merged):
+            top[head, rows] = new_top
+            total[head, rows] = new_total
+            acc[head, rows] = new_acc
 
     def near_attention():
-        @pl.loop(0, heads)
-        def _(head):
-            columns = head_columns(head)
-            raw = scores_of(q_ref[:, columns], k_ref[:, columns])
-            row_top = jnp.max(raw, axis=-1, keepdims=True)
-            weights = jnp.exp((raw - row_top) * scale)
-            top[head] = row_top
-            total[head] = jnp.sum(weights, axis=-1, keepdims=True)
-            acc[head] = jnp.dot(
-                weights.astype(jnp.bfloat16), v_ref[:, columns], preferred_element_type=jnp.float32
-            )
+        @pl.loop(0, heads // 2)
+        def _(index):
+            found = []
+            for head in (index * 2, index * 2 + 1):
+                columns = head_columns(head)
+                raw = scores_of(q_ref[:, columns], k_ref[:, columns])
+                row_top = jnp.max(raw, axis=-1, keepdims=True)
+                weights = jnp.exp((raw - row_top) * scale)
+                row_sum = jnp.sum(weights, axis=-1, keepdims=True)
+                weighted = jnp.dot(
+                    weights.astype(jnp.bfloat16),
+                    v_ref[:, columns],
+                    preferred_element_type=jnp.float32,
+                )
+                found.append((head, row_top, row_sum, weighted))
+            for head, row_top, row_sum, weighted in found:
+                top[head] = row_top
+                total[head] = row_sum
+                acc[head] = weighted
 
     def mark_attention():
-        @pl.loop(0, heads)
-        def _(head):
-            columns = head_columns(head)
-            both = marks[:, :, columns].astype(jnp.float32)
-            mark_keys = both[:, :land].reshape(n_ctx * land, HEAD_DIMENSION).astype(jnp.bfloat16)
-            mark_values = both[:, land:].reshape(n_ctx * land, HEAD_DIMENSION).astype(jnp.bfloat16)
-            merge(head, pl.ds(0, tok_rows), scores_of(q_ref[:, columns], mark_keys), mark_values)
+        @pl.loop(0, heads // 2)
+        def _(index):
+            entries = []
+            for head in (index * 2, index * 2 + 1):
+                columns = head_columns(head)
+                both = marks[:, :, columns].astype(jnp.float32)
+                flat = (n_ctx * land, HEAD_DIMENSION)
+                mark_keys = both[:, :land].reshape(flat).astype(jnp.bfloat16)
+                mark_values = both[:, land:].reshape(flat).astype(jnp.bfloat16)
+                raw = scores_of(q_ref[:, columns], mark_keys)
+                entries.append((head, pl.ds(0, tok_rows), raw, mark_values))
+            merge(entries)
 
     def chosen(ref, wanted, columns):
         picked = ref[pl.ds(0, BLK), columns]
@@ -187,15 +206,20 @@
             if (level, which) != (levels - 1, 0):
                 kv_copies[level, which].wait_recv()
 
-        @pl.loop(0, heads)
-        def _(head):
-            columns = head_columns(head)
-            for block in range(blocks):
-                wanted = pattern_ref[me * blocks + block, NEAR_LEVELS + level] - first
-                rows = pl.ds(block * BLK, BLK)
-                far_keys = chosen(far_k[level], wanted, columns)
-                far_values = chosen(far_v[level], wanted, columns)
-                merge(head, rows, scores_of(q_ref[rows, columns], far_keys), far_values)
+        @pl.loop(0, heads // 4)
+        def _(index):
+            entries = []
+            for extra in range(4):
+                head = index * 4 + extra
+                columns = head_columns(head)
+                for block in range(blocks):
+                    wanted = pattern_ref[me * blocks + block, NEAR_LEVELS + level] - first
+                    rows = pl.ds(block * BLK, BLK)
+                    far_keys = chosen(far_k[level], wanted, columns)
+                    far_values = chosen(far_v[level], wanted, columns)
+                    raw = scores_of(q_ref[rows, columns], far_keys)
+                    entries.append((head, rows, raw, far_values))
+            merge(entries)
 
     half = col_width // 2
     att_copies = {}
@@ -266,48 +290,58 @@
             rows = jnp.dot(attended[index], columns, preferred_element_type=jnp.float32)
             partial[index, turn] = rows.astype(jnp.bfloat16)
 
-    for stage in range(len(order)):
-        for r in held[stage]:
-            project(r)
-    for r in held[len(order)]:
-        for piece in range(PIECES):
-            wait_w(piece, r)
-        project(r)
-
+    my_turn = lax.div(me, GROUP)
+    bits = [1 << bit for bit in range(turns.bit_length() - 1)]
+    low_bits = [bit for bit in bits if bit < share]
     head_copies = {}
-    for index in range(GROUP)[::-1]:
-        for j in range(1, n_head):
-            copy = pltpu.make_async_remote_copy(
-                src_ref=partial.at[index, pl.ds(head_peer[j] * share, share)],
-                dst_ref=arrived.at[j - 1, index],
-                send_sem=head_send.at[j - 1, index],
-                recv_sem=head_recv.at[j - 1, index],
-                device_id={"head": head_peer[j]},
-                device_id_type=MESH,
-            )
-            copy.start()
-            head_copies[index, j] = copy
     out_copies = []
-    for index in range(GROUP)[::-1]:
-        for j in range(1, n_head):
-            head_copies[index, j].wait_recv()
-        target = summed if index else shared
-        for turn in range(share):
+
+    def send_partials(low, turn):
+        for index in range(GROUP)[::-1]:
+            for j in range(1, n_head):
+                copy = pltpu.make_async_remote_copy(
+                    src_ref=partial.at[index, head_peer[j] * share + turn],
+                    dst_ref=arrived.at[j - 1, index, turn],
+                    send_sem=head_send.at[j - 1, index, low],
+                    recv_sem=head_recv.at[j - 1, index, low],
+                    device_id={"head": head_peer[j]},
+                    device_id_type=MESH,
+                )
+                copy.start()
+                head_copies[index, j, low] = copy
+
+    def send_sums(low, turn):
+        for index in range(GROUP)[::-1]:
             mixed = partial[index, my_head * share + turn].astype(jnp.float32)
             for j in range(1, n_head):
+                head_copies[index, j, low].wait_recv()
                 mixed += arrived[j - 1, index, turn].astype(jnp.float32)
+            target = summed if index else shared
             target[index, turn] = mixed.astype(jnp.bfloat16)
-        if index:
-            copy = pltpu.make_async_remote_copy(
-                src_ref=summed.at[index],
-                dst_ref=shared.at[index],
-                send_sem=out_send.at[index],
-                recv_sem=out_recv.at[index],
-                device_id={"ctx": member[index]},
-                device_id_type=MESH,
-            )
-            copy.start()
-            out_copies.append(copy)
+            if index:
+                copy = pltpu.make_async_remote_copy(
+                    src_ref=summed.at[index, turn],
+                    dst_ref=shared.at[index, turn],
+                    send_sem=out_send.at[index, low],
+                    recv_sem=out_recv.at[index, low],
+                    device_id={"ctx": member[index]},
+                    device_id_type=MESH,
+                )
+                copy.start()
+                out_copies.append(copy)
+
+    late = set(held[len(order)])
+    everything = [r for stage in held for r in stage]
+    for low in range(share):
+        turn = differing_bits(lax.rem(my_turn, share), low, low_bits)
+        for r in everything:
+            if (r // GROUP) % share == low:
+                if r in late:
+                    for piece in range(PIECES):
+                        wait_w(piece, r)
+                project(r)
+        send_partials(low, turn)
+        send_sums(low, turn)
     for copy in out_copies:
         copy.wait_recv()
 
@@ -362,10 +396,10 @@
             pltpu.SemaphoreType.DMA((levels,)),
             pltpu.SemaphoreType.DMA((GROUP, 2)),
             pltpu.SemaphoreType.DMA((GROUP, 2)),
-            pltpu.SemaphoreType.DMA((n_head - 1, GROUP)),
-            pltpu.SemaphoreType.DMA((n_head - 1, GROUP)),
-            pltpu.SemaphoreType.DMA((GROUP,)),
-            pltpu.SemaphoreType.DMA((GROUP,)),
+            pltpu.SemaphoreType.DMA((n_head - 1, GROUP, share)),
+            pltpu.SemaphoreType.DMA((n_head - 1, GROUP, share)),
+            pltpu.SemaphoreType.DMA((GROUP, share)),
+            pltpu.SemaphoreType.DMA((GROUP, share)),
         ],
         compiler_params=pltpu.CompilerParams(
             collective_id=0, has_side_effects=True, vmem_limit_bytes=56 * 1024 * 1024

time: 206 us -> 191 us (0.927)
  Pallas kernels: 202 us -> 187 us
    pallas_call x1, Pallas kernels: 202 us -> 187 us  [on_device(): pl.pallas_call(functools.partial(layer_kernel, n_ctx, n_head), out_shape=...]
where the time goes in v3:
time: 191 us
  Pallas kernels  187 us (98%)
  local copies, waits for them, and re-layouts  3.68 us (2%)
    pallas_call x1, Pallas kernels, on_device(): pl.pallas_call(functools.partial(layer_kernel, n_ctx, n_head), out_shape=...  187 us

profile of v3, /device:TPU:11, one launch (start us, length us, event | category | flops | bytes accessed | tf_op | source)
XLA Modules:
  0.0 191.0 jit_solution(7916590260413794076)
XLA Ops:
  0.0 1.4 copy.7.refs_5_
  1.4 187.3 %shard_map.64 = bf16[256,2048]{1,0:T(8,128)(2,1)} custom-call(bf16[256,2048]{1,0:T(8,128)(2,1)} %refs_0_.1, bf16[256,2048]{1,0:T(8,128)(2,1)} %refs_1_.1, bf16[256,2048]{1,0:T(8,128)(2,1)} %refs_2_.1, bf16[8,256]{1,0:T(8,128)(2,1)} %refs_3_.1, bf16[2048,256]{1,0:T(8,128)(2,1)} %refs_4_.1, s32[32,5]{1,0:T(8,128)} %copy.7.refs_5_), custom_call_target="tpu_custom_call" | custom-call | tf_op jit(solution)/shard_map/pallas_call | solution.py:374
  188.7 2.3 %copy.9 = bf16[256,2048]{1,0:T(8,128)(2,1)} copy(bf16[256,2048]{1,0:T(8,128)(2,1)} %shard_map.64) | data formatting | bytes 2097152

commit v4 on v3

--- a/solution.py
+++ b/solution.py
@@ -202,8 +202,8 @@
 
     def far_attention(level):
         first = partner[steps[level]] * blocks
-        for which in range(2):
-            if (level, which) != (levels - 1, 0):
+        if level != levels - 1:
+            for which in range(2):
                 kv_copies[level, which].wait_recv()
 
         @pl.loop(0, heads // 4)
@@ -251,7 +251,8 @@
     send_marks(1)
     far_attention(0)
     far_attention(1)
-    kv_copies[levels - 1, 0].wait_recv()
+    for which in range(2):
+        kv_copies[levels - 1, which].wait_recv()
     for stage in range(len(order)):
         for piece in range(PIECES):
             send_w(piece, 0, stage)

time: 191 us -> 192 us (level)
  no operation moved by 1% of the time
where the time goes in v4:
time: 192 us
  Pallas kernels  188 us (98%)
  local copies, waits for them, and re-layouts  3.68 us (2%)
    pallas_call x1, Pallas kernels, on_device(): pl.pallas_call(functools.partial(layer_kernel, n_ctx, n_head), out_shape=...  188 us

profile of v4, /device:TPU:11, one launch (start us, length us, event | category | flops | bytes accessed | tf_op | source)
XLA Modules:
  0.0 191.8 jit_solution(17419689746732393316)
XLA Ops:
  0.0 1.4 copy.7.refs_5_
  1.4 188.1 %shard_map.64 = bf16[256,2048]{1,0:T(8,128)(2,1)} custom-call(bf16[256,2048]{1,0:T(8,128)(2,1)} %refs_0_.1, bf16[256,2048]{1,0:T(8,128)(2,1)} %refs_1_.1, bf16[256,2048]{1,0:T(8,128)(2,1)} %refs_2_.1, bf16[8,256]{1,0:T(8,128)(2,1)} %refs_3_.1, bf16[2048,256]{1,0:T(8,128)(2,1)} %refs_4_.1, s32[32,5]{1,0:T(8,128)} %copy.7.refs_5_), custom_call_target="tpu_custom_call" | custom-call | tf_op jit(solution)/shard_map/pallas_call | solution.py:375
  189.5 2.3 %copy.9 = bf16[256,2048]{1,0:T(8,128)(2,1)} copy(bf16[256,2048]{1,0:T(8,128)(2,1)} %shard_map.64) | data formatting | bytes 2097152

commit v5 on v3

--- a/solution.py
+++ b/solution.py
@@ -37,13 +37,13 @@
 def layer_kernel(n_ctx, n_head, *refs):
     steps = [1 << bit for bit in range(n_ctx.bit_length() - 1)]
     levels = len(steps)
-    q_ref, k_ref, v_ref, pool_ref, w_ref, pattern_ref, out_ref = refs[:7]
-    refs = refs[7:]
+    q_ref, k_hbm, v_hbm, pool_ref, w_ref, pattern_ref, out_ref, k_ref, v_ref = refs[:9]
+    refs = refs[9:]
     far_k, refs = refs[:levels], refs[levels:]
     far_v, refs = refs[:levels], refs[levels:]
     (w_buf, marks, acc, top, total, attended, partial, arrived, summed, shared) = refs[:10]
     (kv_send, kv_recv, w_send, w_recv, mark_send, mark_recv) = refs[10:16]
-    (att_send, att_recv, head_send, head_recv, out_send, out_recv) = refs[16:]
+    (att_send, att_recv, head_send, head_recv, out_send, out_recv, near_sem) = refs[16:]
 
     tok_rows, col_width = q_ref.shape
     heads = col_width // HEAD_DIMENSION
@@ -111,7 +111,7 @@
     kv_copies = {}
 
     def send_kv(level, which):
-        source, target = ((k_ref, far_k[level]), (v_ref, far_v[level]))[which]
+        source, target = ((k_hbm, far_k[level]), (v_hbm, far_v[level]))[which]
         copy = pltpu.make_async_remote_copy(
             src_ref=source,
             dst_ref=target,
@@ -237,16 +237,30 @@
         copy.start()
         att_copies[source ^ step, piece] = copy
 
+    for level in range(2, levels)[::-1]:
+        send_kv(level, 0)
+    near_copies = [
+        pltpu.make_async_copy(source, target, near_sem.at[which])
+        for which, (source, target) in enumerate(((k_hbm, k_ref), (v_hbm, v_ref)))
+    ]
+    for copy in near_copies:
+        copy.start()
+    for level in range(2):
+        send_kv(level, 0)
+    for copy in near_copies:
+        copy.wait()
     pooled = [
         jnp.dot(pool_ref[...], ref[...], preferred_element_type=jnp.float32) for ref in (k_ref, v_ref)
     ]
     marks[0] = jnp.concatenate(pooled, axis=0).astype(jnp.bfloat16)
     send_marks(0)
-    for which in range(2):
-        for level in range(levels)[::-1]:
-            send_kv(level, which)
-
+    for level in range(levels)[::-1]:
+        send_kv(level, 1)
+
+    own_copy = pltpu.make_async_copy(w_ref, w_buf.at[0], near_sem.at[2])
+    own_copy.start()
     near_attention()
+    own_copy.wait()
     mark_copies[0].wait_recv()
     send_marks(1)
     far_attention(0)
@@ -286,8 +300,9 @@
 
         @pl.loop(0, GROUP)
         def _(index):
-            columns = w_ref[...] if r == 0 else w_buf[r // GROUP]
-            rows = jnp.dot(attended[index], columns, preferred_element_type=jnp.float32)
+            rows = jnp.dot(
+                attended[index], w_buf[r // GROUP], preferred_element_type=jnp.float32
+            )
             partial[index, turn] = rows.astype(jnp.bfloat16)
 
     my_turn = lax.div(me, GROUP)
@@ -371,12 +386,14 @@
     share = turns // n_head
     bf16 = jnp.bfloat16
     in_vmem = pl.BlockSpec(memory_space=pltpu.VMEM)
+    in_place = pl.BlockSpec(memory_space=pl.ANY)
     return pl.pallas_call(
         functools.partial(layer_kernel, n_ctx, n_head),
         out_shape=jax.ShapeDtypeStruct((tok_rows, share * GROUP * w_width), bf16),
-        in_specs=[in_vmem] * 5 + [pl.BlockSpec(memory_space=pltpu.SMEM)],
+        in_specs=[in_vmem, in_place, in_place, in_vmem, in_place]
+        + [pl.BlockSpec(memory_space=pltpu.SMEM)],
         out_specs=in_vmem,
-        scratch_shapes=[pltpu.VMEM((tok_rows, col_width), bf16)] * (2 * levels)
+        scratch_shapes=[pltpu.VMEM((tok_rows, col_width), bf16)] * (2 * levels + 2)
         + [
             pltpu.VMEM((turns, depth, w_width), bf16),
             pltpu.VMEM((n_ctx, 2 * land, col_width), bf16),
@@ -400,6 +417,7 @@
             pltpu.SemaphoreType.DMA((n_head - 1, GROUP, share)),
             pltpu.SemaphoreType.DMA((GROUP, share)),
             pltpu.SemaphoreType.DMA((GROUP, share)),
+            pltpu.SemaphoreType.DMA((3,)),
         ],
         compiler_params=pltpu.CompilerParams(
             collective_id=0, has_side_effects=True, vmem_limit_bytes=56 * 1024 * 1024

time: 191 us -> 190 us (level)
  no operation moved by 1% of the time
where the time goes in v5:
time: 190 us
  Pallas kernels  186 us (98%)
  local copies, waits for them, and re-layouts  3.68 us (2%)
    pallas_call x1, Pallas kernels, on_device(): pl.pallas_call(functools.partial(layer_kernel, n_ctx, n_head), out_shape=...  186 us

profile of v5, /device:TPU:11, one launch (start us, length us, event | category | flops | bytes accessed | tf_op | source)
XLA Modules:
  0.0 189.6 jit_solution(3373984391867536391)
XLA Ops:
  0.0 1.4 copy.7.refs_5_
  1.4 185.9 %shard_map.64 = bf16[256,2048]{1,0:T(8,128)(2,1)} custom-call(bf16[256,2048]{1,0:T(8,128)(2,1)} %refs_0_.1, bf16[256,2048]{1,0:T(8,128)(2,1)} %refs_1_.1, bf16[256,2048]{1,0:T(8,128)(2,1)} %refs_2_.1, bf16[8,256]{1,0:T(8,128)(2,1)} %refs_3_.1, bf16[2048,256]{1,0:T(8,128)(2,1)} %refs_4_.1, s32[32,5]{1,0:T(8,128)} %copy.7.refs_5_), custom_call_target="tpu_custom_call" | custom-call | tf_op jit(solution)/shard_map/pallas_call | solution.py:390
  187.3 2.3 %copy.9 = bf16[256,2048]{1,0:T(8,128)(2,1)} copy(bf16[256,2048]{1,0:T(8,128)(2,1)} %shard_map.64) | data formatting | bytes 2097152

commit v6 on v5

--- a/solution.py
+++ b/solution.py
@@ -295,15 +295,15 @@
     turns = n_ctx // GROUP
     share = turns // n_head
 
+    def project_rows(r, index):
+        turn = lax.div(differing_bits(me, r, steps), GROUP)
+        rows = jnp.dot(attended[index], w_buf[r // GROUP], preferred_element_type=jnp.float32)
+        partial[index, turn] = rows.astype(jnp.bfloat16)
+
     def project(r):
-        turn = lax.div(differing_bits(me, r, steps), GROUP)
-
         @pl.loop(0, GROUP)
         def _(index):
-            rows = jnp.dot(
-                attended[index], w_buf[r // GROUP], preferred_element_type=jnp.float32
-            )
-            partial[index, turn] = rows.astype(jnp.bfloat16)
+            project_rows(r, index)
 
     my_turn = lax.div(me, GROUP)
     bits = [1 << bit for bit in range(turns.bit_length() - 1)]
@@ -311,8 +311,9 @@
     head_copies = {}
     out_copies = []
 
-    def send_partials(low, turn):
+    def send_partials(low, turn, last):
         for index in range(GROUP)[::-1]:
+            project_rows(last, index)
             for j in range(1, n_head):
                 copy = pltpu.make_async_remote_copy(
                     src_ref=partial.at[index, head_peer[j] * share + turn],
@@ -349,13 +350,14 @@
     everything = [r for stage in held for r in stage]
     for low in range(share):
         turn = differing_bits(lax.rem(my_turn, share), low, low_bits)
-        for r in everything:
-            if (r // GROUP) % share == low:
-                if r in late:
-                    for piece in range(PIECES):
-                        wait_w(piece, r)
+        wanted_now = [r for r in everything if (r // GROUP) % share == low]
+        for r in wanted_now:
+            if r in late:
+                for piece in range(PIECES):
+                    wait_w(piece, r)
+            if r != wanted_now[-1]:
                 project(r)
-        send_partials(low, turn)
+        send_partials(low, turn, wanted_now[-1])
         send_sums(low, turn)
     for copy in out_copies:
         copy.wait_recv()

time: 190 us -> 189 us (level)
  Pallas kernels: 186 us -> 184 us
where the time goes in v6:
time: 189 us; the launch traced here: 188 us
  Pallas kernels  184 us (97%)
  local copies, waits for them, and re-layouts  3.68 us (2%)
    pallas_call x1, Pallas kernels, on_device(): pl.pallas_call(functools.partial(layer_kernel, n_ctx, n_head), out_shape=...  184 us

profile of v6, /device:TPU:11, one launch (start us, length us, event | category | flops | bytes accessed | tf_op | source)
XLA Modules:
  0.0 187.8 jit_solution(14967445449476601523)
XLA Ops:
  0.0 1.4 copy.7.refs_5_
  1.4 184.1 %shard_map.64 = bf16[256,2048]{1,0:T(8,128)(2,1)} custom-call(bf16[256,2048]{1,0:T(8,128)(2,1)} %refs_0_.1, bf16[256,2048]{1,0:T(8,128)(2,1)} %refs_1_.1, bf16[256,2048]{1,0:T(8,128)(2,1)} %refs_2_.1, bf16[8,256]{1,0:T(8,128)(2,1)} %refs_3_.1, bf16[2048,256]{1,0:T(8,128)(2,1)} %refs_4_.1, s32[32,5]{1,0:T(8,128)} %copy.7.refs_5_), custom_call_target="tpu_custom_call" | custom-call | tf_op jit(solution)/shard_map/pallas_call | solution.py:392
  185.5 2.3 %copy.9 = bf16[256,2048]{1,0:T(8,128)(2,1)} copy(bf16[256,2048]{1,0:T(8,128)(2,1)} %shard_map.64) | data formatting | bytes 2097152
